TPU v7x, 256 devices: a whole 4x4x8 slice. The times are simulated.
256 devices in a mesh: dp: 32 (over y, x, core), fsdp: 8 (over z).
Axes of the slice: x: 4, y: 4, z: 8, core: 2. Of those that a mesh axis runs over, the one named last changes fastest.
Arguments:
- hidden: bfloat16 [65536, 8192], P('dp', 'fsdp'), may hold values from -50 to 50
- logit_grad: bfloat16 [65536, 1024], P('dp'), may hold values from -20 to 20
- master: float32 [1024, 8192], P('dp', 'fsdp'), may hold values from -6 to 6
- moment_one: float32 [1024, 8192], P('dp', 'fsdp'), may hold values from -4 to 4
- moment_two: float32 [1024, 8192], P('dp', 'fsdp'), may hold values from 0.25 to 4
Outputs:
- new_rows: bfloat16 [1024, 8192], P(None, 'fsdp')
- new_master: float32 [1024, 8192], P('dp', 'fsdp')
- new_one: float32 [1024, 8192], P('dp', 'fsdp')
- new_two: float32 [1024, 8192], P('dp', 'fsdp')
All inputs are finite; a program needn't handle non-finite values.
Results may differ from a plain program's by a relative error of at most 0.012.
Values may be sent and summed in bfloat16 or wider, within the bound.
No kernel may reach another device: no remote copies, remote signals or barrier semaphores. Data moves between devices by JAX's collectives and lax.ppermute only.
A program may use at most 64 MiB of HBM per device.

v0:
```python
import functools

import jax
import jax.numpy as jnp
from jax import lax
from jax.experimental import pallas as pl
from jax.experimental.pallas import tpu as pltpu
from jax.sharding import Mesh
from jax.sharding import PartitionSpec as P

CHIPS = ("dp_0", "dp_1")
CORE = "dp_2"
DP = (*CHIPS, CORE)
SIDE = 4
SWAP = [(0, 1), (1, 0)]
VMEM = pl.BlockSpec(memory_space=pltpu.VMEM)
HBM = pl.BlockSpec(memory_space=pl.ANY)
BF16, F32 = jnp.bfloat16, jnp.float32


def near(value):
    return pltpu.with_memory_space_constraint(value, pltpu.VMEM)


def far(value):
    return pltpu.with_memory_space_constraint(value, pltpu.HBM)


def call(body, outs, args, flops=0, moved=0, specs=None, out_specs=None, **more):
    return pl.pallas_call(
        body,
        out_shape=outs,
        in_specs=specs or [VMEM] * len(args),
        out_specs=out_specs or [VMEM] * len(outs),
        cost_estimate=pl.CostEstimate(flops=flops, bytes_accessed=moved, transcendentals=0),
        compiler_params=pltpu.CompilerParams(vmem_limit_bytes=24 * 2**20),
        **more,
    )(*args)


def product(left, right):
    return lax.dot_general(left, right, (((0,), (0,)), ((), ())), preferred_element_type=F32)


def core_columns(half):
    here = lax.axis_index(CORE)
    own = pl.ds(pl.multiple_of(here * half, half), half)
    return own, pl.ds(pl.multiple_of((1 - here) * half, half), half)


def pieces(core, distant):
    row, column = (lax.axis_index(axis) for axis in CHIPS)
    pair = lax.bitwise_xor(lax.shift_right_logical(jnp.where(core == 0, column, row), 1), distant)
    starts = [
        jnp.where(core == 0, 256 * part + 128 * pair, 512 * pair + 128 * part)
        for part in range(SIDE)
    ]
    return [pl.ds(pl.multiple_of(start, 128), 128) for start in starts]


def load_and_multiply(chunks, lg_hbm, hid_hbm, lg, mine, distant, close, theirs, total, sems):
    tokens = lg.shape[0]
    step = tokens // chunks
    own, other = core_columns(mine.shape[1])
    copies = []
    for k in range(chunks):
        part = pl.ds(k * step, step)
        copies.append(
            (
                pltpu.make_async_copy(lg_hbm.at[part], lg.at[part], sems.at[k, 0]),
                pltpu.make_async_copy(hid_hbm.at[part, other], theirs.at[part], sems.at[k, 1]),
            )
        )
        for copy in copies[-1]:
            copy.start()
    last = pltpu.make_async_copy(hid_hbm.at[:, own], mine, sems.at[chunks, 0])
    last.start()
    core = 1 - lax.axis_index(CORE)
    for k in range(chunks):
        part = pl.ds(k * step, step)
        for copy in copies[k]:
            copy.wait()
        for number, out in ((1, distant), (0, close)):
            for place, block in enumerate(pieces(core, number)):
                here, there = pl.ds(512 * number + 128 * place, 128), pl.ds(128 * place, 128)
                value = product(lg[part, block], theirs[part, :])
                if k > 0:
                    value += total[here, :]
                if k < chunks - 1:
                    total[here, :] = value
                else:
                    out[there, :] = value.astype(BF16)
    last.wait()


def multiply(distant, lg, hid, out):
    for place, block in enumerate(pieces(lax.axis_index(CORE), distant)):
        out[pl.ds(128 * place, 128), :] = product(lg[:, block], hid[...]).astype(BF16)


def arrange(distant, kept, arrived, *outs):
    here, row, column = (lax.axis_index(axis) for axis in (CORE, *CHIPS))
    size = outs[0].shape[1]
    for mask, out in enumerate(outs):
        low = lax.bitwise_xor(jnp.where(here == 0, column, row), mask) & 1
        for place in range(SIDE):
            block = jnp.where(here == 0, 2 * place + low, SIDE * low + place)
            rows = pl.ds(pl.multiple_of(block * size, size), size)
            out[place] = (kept[rows, :].astype(F32) + arrived[rows, :].astype(F32)).astype(BF16)


def add_first(own, one, two, three, *outs):
    here, row, column = (lax.axis_index(axis) for axis in (CORE, *CHIPS))
    second = jnp.where(here == 0, row, column)
    for mask, out in enumerate(outs):
        place = lax.bitwise_xor(second, mask)
        total = own[place].astype(F32) + one[place].astype(F32)
        total += two[place].astype(F32) + three[place].astype(F32)
        out[...] = total.astype(out.dtype)


def add_second(own, one, two, three, grad, squares):
    value = own[...] + one[...].astype(F32) + two[...].astype(F32) + three[...].astype(F32)
    grad[...] = value
    square = value * value
    lanes = sum(square[:, first : first + 128] for first in range(0, value.shape[1], 128))
    squares[...] = jnp.broadcast_to(jnp.sum(lanes, axis=0, keepdims=True)[None], squares.shape)


def pack(*refs):
    (*sources, out) = refs
    _, other = core_columns(out.shape[2])
    for number, source in enumerate(sources):
        out[number] = source[:, other]


def update(entries, sums, grad, master, moment_one, moment_two, packed, values, kept, sent):
    here = lax.axis_index(CORE)
    rows, half = kept.shape[1:]
    own, _ = core_columns(half)
    sumsq = jnp.sum(jnp.sum(sums[...], axis=0, keepdims=True), axis=1, keepdims=True)
    factor = jnp.minimum(1.0, 1.0 / jnp.sqrt(sumsq / entries))
    owned = (master[:, own], moment_one[:, own], moment_two[:, own])
    lent = (packed[0], packed[1], packed[2])
    for core, (old, old_one, old_two), out in ((here, owned, kept), (1 - here, lent, sent)):
        place = pl.ds(pl.multiple_of(core * rows, rows), rows)
        clipped = factor * grad[place, :]
        one = 0.9 * old_one + 0.1 * clipped
        two = 0.95 * old_two + 0.05 * clipped * clipped
        first = one / (1.0 - 0.9**10)
        second = two / (1.0 - 0.95**10)
        value = old - 0.05 * (first / (jnp.sqrt(second) + 1e-08) + 0.1 * old)
        out[0], out[1], out[2] = value, one, two
        values[place, :] = value.astype(BF16)


def join(*refs):
    (*sources, out) = refs
    for number, source in enumerate(sources):
        out[number] = source[...]


def row_copies(source, second_mask, core, out, sems, number):
    row, column = (lax.axis_index(axis) for axis in CHIPS)
    size, half = source.shape[1:]
    columns = pl.ds(pl.multiple_of(core * half, half), half)
    copies = []
    for mask in range(SIDE):
        chip = jnp.where(
            core == 0,
            lax.bitwise_xor(row, mask) * SIDE + lax.bitwise_xor(column, second_mask),
            lax.bitwise_xor(row, second_mask) * SIDE + lax.bitwise_xor(column, mask),
        )
        rows = pl.ds(pl.multiple_of(chip * size, size), size)
        copies.append(
            pltpu.make_async_copy(source.at[mask], out.at[rows, columns], sems.at[number + mask])
        )
    return copies


def write_first(own, arrived, kept, given, out, new_master, new_one, new_two, sems):
    here = lax.axis_index(CORE)
    copies = row_copies(own, 0, here, out, sems, 0)
    copies += row_copies(arrived, 0, 1 - here, out, sems, len(copies))
    for source, columns in zip((kept, given), core_columns(kept.shape[2])):
        for number, target in enumerate((new_master, new_one, new_two)):
            copies.append(
                pltpu.make_async_copy(
                    source.at[number], target.at[:, columns], sems.at[len(copies)]
                )
            )
    for copy in copies:
        copy.start()
    for copy in copies:
        copy.wait()


def write_rest(other, *refs):
    (*sources, _, out, sems) = refs
    here = lax.axis_index(CORE)
    core = 1 - here if other else here
    copies = []
    for mask, source in enumerate(sources, 1):
        copies += row_copies(source, mask, core, out, sems, len(copies))
    for copy in copies:
        copy.start()
    for copy in copies:
        copy.wait()


def partners(mask, stage):
    pairs = []
    for row in range(SIDE):
        for column in range(SIDE):
            for core in range(2):
                place = (row * SIDE + column) * 2 + core
                if core == stage:
                    other = (row * SIDE + (column ^ mask)) * 2 + core
                else:
                    other = ((row ^ mask) * SIDE + column) * 2 + core
                pairs.append((place, other))
    return pairs


def shards(hidden, logit_grad, master, moment_one, moment_two):
    rows, columns = master.shape
    tokens, total_rows = logit_grad.shape
    half = columns // 2
    everyone = (*DP, "fsdp")
    count = lax.axis_size(everyone)
    width = columns * lax.axis_size("fsdp")
    work = 2 * tokens * total_rows * half

    chunks = 4
    lg, mine, *sent = call(
        functools.partial(load_and_multiply, chunks),
        [
            pltpu.VMEM((tokens, total_rows), BF16),
            pltpu.VMEM((tokens, half), BF16),
            pltpu.VMEM((total_rows // 2, half), BF16),
            pltpu.VMEM((total_rows // 2, half), BF16),
        ],
        [far(logit_grad), far(hidden)],
        flops=work,
        moved=4 * tokens * columns,
        specs=[HBM, HBM],
        scratch_shapes=[
            pltpu.VMEM((tokens, half), BF16),
            pltpu.VMEM((total_rows, half), F32),
            pltpu.SemaphoreType.DMA((chunks + 1, 2)),
        ],
    )
    blocks = []
    for distant, value in zip((1, 0), sent):
        arrived = lax.ppermute(value, CORE, SWAP)
        (kept,) = call(
            functools.partial(multiply, distant),
            [pltpu.VMEM((total_rows // 2, half), BF16)],
            [near(lg), near(mine)],
            flops=work // 2,
            moved=tokens * columns,
        )
        blocks = [
            *call(
                functools.partial(arrange, distant),
                [pltpu.VMEM((SIDE, 2 * rows, half), BF16)] * 2,
                [near(kept), near(arrived)],
            ),
            *blocks,
        ]
    first = [blocks[0]] + [
        lax.ppermute(blocks[mask], DP, partners(mask, 0)) for mask in (2, 3, 1)
    ]
    *states, _ = lax.optimization_barrier((master, moment_one, moment_two, first[1]))
    (lent,) = call(
        pack, [pltpu.VMEM((3, rows, half), F32)], [near(state) for state in states]
    )
    packed = lax.ppermute(lent, CORE, SWAP)
    totals = call(
        add_first,
        [pltpu.VMEM((2 * rows, half), F32)] + [pltpu.VMEM((2 * rows, half), BF16)] * (SIDE - 1),
        [near(value) for value in first],
    )
    second = [totals[0]] + [
        lax.ppermute(totals[mask], DP, partners(mask, 1)) for mask in (2, 1, 3)
    ]
    grad, copies = call(
        add_second,
        [pltpu.VMEM((2 * rows, half), F32), pltpu.VMEM((count, 1, 128), F32)],
        [near(value) for value in second],
    )
    copies, packed = lax.optimization_barrier((copies, packed))
    sums = lax.all_to_all(copies, everyone, 0, 0, tiled=True).reshape(count, 128)

    values, kept, sent = call(
        functools.partial(update, float(total_rows * width)),
        [pltpu.VMEM((2 * rows, half), BF16)] + [pltpu.VMEM((3, rows, half), F32)] * 2,
        [near(value) for value in (sums, grad, *states, packed)],
    )
    line = {mask: lax.ppermute(values, DP, partners(mask, 1)) for mask in (1, 3, 2)}
    line = [values] + [line[mask] for mask in range(1, SIDE)]
    (joined,) = call(
        join, [pltpu.VMEM((SIDE, 2 * rows, half), BF16)], [near(value) for value in line]
    )
    given = lax.ppermute(sent, CORE, SWAP)
    plane = {mask: lax.ppermute(joined, DP, partners(mask, 0)) for mask in (1, 3, 2)}
    plane = [joined] + [plane[mask] for mask in range(1, SIDE)]
    plane[2], given = lax.optimization_barrier((plane[2], given))
    across = lax.ppermute(joined, CORE, SWAP)
    slab = pltpu.HBM((total_rows, columns), BF16)
    new_rows, new_master, new_one, new_two = call(
        write_first,
        [slab] + [pltpu.HBM((rows, columns), F32)] * 3,
        [near(value) for value in (joined, across, kept, given)],
        moved=total_rows * columns,
        out_specs=[HBM] * 4,
        scratch_shapes=[pltpu.SemaphoreType.DMA((2 * SIDE + 6,))],
    )
    plane[1], new_rows = lax.optimization_barrier((plane[1], new_rows))
    others = [lax.ppermute(value, CORE, SWAP) for value in plane[1:]]
    for other, sources in enumerate((plane[1:], others)):
        (new_rows,) = call(
            functools.partial(write_rest, other),
            [slab],
            [*(near(value) for value in sources), far(new_rows)],
            moved=total_rows * columns,
            specs=[VMEM] * (SIDE - 1) + [HBM],
            out_specs=[HBM],
            scratch_shapes=[pltpu.SemaphoreType.DMA((SIDE * (SIDE - 1),))],
            input_output_aliases={SIDE - 1: 0},
        )
    return (new_rows, new_master, new_one, new_two)


def solution(mesh):
    torus = Mesh(
        mesh.devices.reshape(SIDE, SIDE, 2, mesh.shape["fsdp"]), (*DP, "fsdp")
    )
    placed = (P(DP, "fsdp"), P(DP, None), P(DP, "fsdp"), P(DP, "fsdp"), P(DP, "fsdp"))
    return jax.shard_map(
        shards,
        mesh=torus,
        in_specs=placed,
        out_specs=(P(None, "fsdp"), P(DP, "fsdp"), P(DP, "fsdp"), P(DP, "fsdp")),
        check_vma=False,
    )
```

profile of v0, /device:TPU:1, one launch (start us, length us, event | category | flops | bytes accessed | tf_op | source)
XLA Modules:
  0.0 75.1 jit_solution(12616361159213094538)
XLA Ops:
  0.6 4.2 %shard_map.84 = (bf16[2048,1024]{1,0:T(8,128)(2,1)S(1)}, bf16[2048,512]{1,0:T(8,128)(2,1)S(1)}, bf16[512,512]{1,0:T(8,128)(2,1)S(1)}, bf16[512,512]{1,0:T(8,128)(2,1)S(1)}) custom-call(bf16[2048,1024]{1,0:T(8,128)(2,1)} %lg_hbm.1, bf16[2048,1024]{1,0:T(8,128)(2,1)} %hid_hbm.1), custom_call_target="tpu_custom_call" | custom-call | flops 2147483648 | bytes 8388608 | tf_op jit(solution)/shard_map/pallas_call | solution.py:30
  4.9 3.4 %collective-permute-start.1 = (bf16[512,512]{1,0:T(8,128)(2,1)S(1)}, bf16[512,512]{1,0:T(8,128)(2,1)S(1)}, u32[]{:S(2)}, u32[]{:S(2)}) collective-permute-start(bf16[512,512]{1,0:T(8,128)(2,1)S(1)} %get-tuple-element.38), channel_id=1, source_target_pairs={{0,8},{8,0},{1,9},{9,1},{2,10},{10,2},{3,11},{11,3},{4,12},{12,4},... | collective-permute-start | bytes 1572872 | tf_op jit(solution)/shard_map/ppermute | solution.py:255
  8.4 1.4 %shard_map.87.kept = bf16[512,512]{1,0:T(8,128)(2,1)S(1)} custom-call(bf16[2048,1024]{1,0:T(8,128)(2,1)S(1)} %get-tuple-element.34.lg, bf16[2048,512]{1,0:T(8,128)(2,1)S(1)} %get-tuple-element.35.hid), custom_call_target="tpu_custom_call" | custom-call | flops 1073741824 | bytes 2097152 | tf_op jit(solution)/shard_map/pallas_call | solution.py:30
  10.0 1.2 %collective-permute-start.2 = (bf16[4,64,512]{2,1,0:T(8,128)(2,1)S(1)}, bf16[4,64,512]{2,1,0:T(8,128)(2,1)S(1)}, u32[]{:S(2)}, u32[]{:S(2)}) collective-permute-start(bf16[4,64,512]{2,1,0:T(8,128)(2,1)S(1)} %get-tuple-element.39), channel_id=1, source_target_pairs={{0,32},{8,136},{16,48},{24,152},{32,0},{40,168},{48,16},{56,184},{... | collective-permute-start | bytes 786440 | tf_op jit(solution)/shard_map/ppermute | solution.py:272
  11.2 1.4 %shard_map.85.kept = bf16[512,512]{1,0:T(8,128)(2,1)S(1)} custom-call(bf16[2048,1024]{1,0:T(8,128)(2,1)S(1)} %get-tuple-element.34.lg, bf16[2048,512]{1,0:T(8,128)(2,1)S(1)} %get-tuple-element.35.hid), custom_call_target="tpu_custom_call" | custom-call | flops 1073741824 | bytes 2097152 | tf_op jit(solution)/shard_map/pallas_call | solution.py:30
  13.2 1.7 %collective-permute-start.3 = (bf16[4,64,512]{2,1,0:T(8,128)(2,1)S(1)}, bf16[4,64,512]{2,1,0:T(8,128)(2,1)S(1)}, u32[]{:S(2)}, u32[]{:S(2)}) collective-permute-start(bf16[4,64,512]{2,1,0:T(8,128)(2,1)S(1)} %get-tuple-element.40), channel_id=1, source_target_pairs={{0,48},{8,200},{16,32},{24,216},{32,16},{40,232},{48,0},{56,248},{... | collective-permute-start | bytes 786440 | tf_op jit(solution)/shard_map/ppermute | solution.py:272
  14.9 2.1 %collective-permute-done.2.one = bf16[4,64,512]{2,1,0:T(8,128)(2,1)S(1)} collective-permute-done((bf16[4,64,512]{2,1,0:T(8,128)(2,1)S(1)}, bf16[4,64,512]{2,1,0:T(8,128)(2,1)S(1)}, u32[]{:S(2)}, u32[]{:S(2)}) %collective-permute-start.2) | collective-permute-done | bytes 262176 | tf_op jit(solution)/shard_map/ppermute | solution.py:272
  17.1 1.4 %collective-permute-start.8 = (f32[3,32,512]{2,1,0:T(8,128)S(1)}, f32[3,32,512]{2,1,0:T(8,128)S(1)}, u32[]{:S(2)}, u32[]{:S(2)}) collective-permute-start(f32[3,32,512]{2,1,0:T(8,128)S(1)} %shard_map.91), channel_id=1, source_target_pairs={{0,8},{8,0},{1,9},{9,1},{2,10},{10,2},{3,11},{11,3},{4,12},{12,4},... | collective-permute-start | bytes 589832 | tf_op jit(solution)/shard_map/ppermute | solution.py:278
  18.5 1.5 %collective-permute-done.3.two = bf16[4,64,512]{2,1,0:T(8,128)(2,1)S(1)} collective-permute-done((bf16[4,64,512]{2,1,0:T(8,128)(2,1)S(1)}, bf16[4,64,512]{2,1,0:T(8,128)(2,1)S(1)}, u32[]{:S(2)}, u32[]{:S(2)}) %collective-permute-start.3) | collective-permute-done | bytes 262176 | tf_op jit(solution)/shard_map/ppermute | solution.py:272
  20.1 2.6 %collective-permute-start.5 = (bf16[64,512]{1,0:T(8,128)(2,1)S(1)}, bf16[64,512]{1,0:T(8,128)(2,1)S(1)}, u32[]{:S(2)}, u32[]{:S(2)}) collective-permute-start(bf16[64,512]{1,0:T(8,128)(2,1)S(1)} %get-tuple-element.43), channel_id=1, source_target_pairs={{0,128},{8,40},{16,144},{24,56},{32,160},{40,8},{48,176},{56,24},{... | collective-permute-start | bytes 196616 | tf_op jit(solution)/shard_map/ppermute | solution.py:285
  23.5 1.3 %collective-permute-done.5.one = bf16[64,512]{1,0:T(8,128)(2,1)S(1)} collective-permute-done((bf16[64,512]{1,0:T(8,128)(2,1)S(1)}, bf16[64,512]{1,0:T(8,128)(2,1)S(1)}, u32[]{:S(2)}, u32[]{:S(2)}) %collective-permute-start.5) | collective-permute-done | bytes 65568 | tf_op jit(solution)/shard_map/ppermute | solution.py:285
  24.8 1.3 %collective-permute-done.6.two = bf16[64,512]{1,0:T(8,128)(2,1)S(1)} collective-permute-done((bf16[64,512]{1,0:T(8,128)(2,1)S(1)}, bf16[64,512]{1,0:T(8,128)(2,1)S(1)}, u32[]{:S(2)}, u32[]{:S(2)}) %collective-permute-start.6) | collective-permute-done | bytes 65568 | tf_op jit(solution)/shard_map/ppermute | solution.py:285
  26.1 1.5 %collective-permute-done.7.three = bf16[64,512]{1,0:T(8,128)(2,1)S(1)} collective-permute-done((bf16[64,512]{1,0:T(8,128)(2,1)S(1)}, bf16[64,512]{1,0:T(8,128)(2,1)S(1)}, u32[]{:S(2)}, u32[]{:S(2)}) %collective-permute-start.7) | collective-permute-done | bytes 65568 | tf_op jit(solution)/shard_map/ppermute | solution.py:285
  27.7 25.8 %all_to_all.5 = f32[256,1,128]{2,1,0:T(1,128)S(1)} all-to-all(f32[256,1,128]{2,1,0:T(1,128)S(1)} %get-tuple-element.50), channel_id=1, replica_groups=mesh['dp_0'=4,'dp_1'=4,'dp_2'=2,'fsdp'=8] {'dp_0','dp_1','dp_2','fsdp'}, dimensions={0} | all-to-all | bytes 262144 | tf_op jit(solution)/shard_map/all_to_all | solution.py:293
  54.7 1.4 %collective-permute-start.10 = (bf16[64,512]{1,0:T(8,128)(2,1)S(1)}, bf16[64,512]{1,0:T(8,128)(2,1)S(1)}, u32[]{:S(2)}, u32[]{:S(2)}) collective-permute-start(bf16[64,512]{1,0:T(8,128)(2,1)S(1)} %get-tuple-element.53.refs_0_), channel_id=1, source_target_pairs={{0,128},{8,40},{16,144},{24,56},{32,160},{40,8},{48,176},{56,24},{... | collective-permute-start | bytes 196616 | tf_op jit(solution)/shard_map/ppermute | solution.py:300
  56.1 1.2 %collective-permute-start.9 = (bf16[64,512]{1,0:T(8,128)(2,1)S(1)}, bf16[64,512]{1,0:T(8,128)(2,1)S(1)}, u32[]{:S(2)}, u32[]{:S(2)}) collective-permute-start(bf16[64,512]{1,0:T(8,128)(2,1)S(1)} %get-tuple-element.53.refs_0_), channel_id=1, source_target_pairs={{0,64},{8,24},{16,80},{24,8},{32,96},{40,56},{48,112},{56,40},{64,... | collective-permute-start | bytes 196616 | tf_op jit(solution)/shard_map/ppermute | solution.py:300
  57.3 1.1 %collective-permute-done.11.refs_3_ = bf16[64,512]{1,0:T(8,128)(2,1)S(1)} collective-permute-done((bf16[64,512]{1,0:T(8,128)(2,1)S(1)}, bf16[64,512]{1,0:T(8,128)(2,1)S(1)}, u32[]{:S(2)}, u32[]{:S(2)}) %collective-permute-start.11) | collective-permute-done | bytes 65568 | tf_op jit(solution)/shard_map/ppermute | solution.py:300
  60.5 2.1 %collective-permute-start.13 = (bf16[4,64,512]{2,1,0:T(8,128)(2,1)S(1)}, bf16[4,64,512]{2,1,0:T(8,128)(2,1)S(1)}, u32[]{:S(2)}, u32[]{:S(2)}) collective-permute-start(bf16[4,64,512]{2,1,0:T(8,128)(2,1)S(1)} %shard_map.93.own), channel_id=1, source_target_pairs={{0,8},{8,0},{1,9},{9,1},{2,10},{10,2},{3,11},{11,3},{4,12},{12,4},... | collective-permute-start | bytes 786440 | tf_op jit(solution)/shard_map/ppermute | solution.py:309
  62.7 1.0 %collective-permute-start.12 = (bf16[4,64,512]{2,1,0:T(8,128)(2,1)S(1)}, bf16[4,64,512]{2,1,0:T(8,128)(2,1)S(1)}, u32[]{:S(2)}, u32[]{:S(2)}) collective-permute-start(bf16[4,64,512]{2,1,0:T(8,128)(2,1)S(1)} %shard_map.93.own), channel_id=1, source_target_pairs={{0,16},{8,72},{16,0},{24,88},{32,48},{40,104},{48,32},{56,120},{64... | collective-permute-start | bytes 786440 | tf_op jit(solution)/shard_map/ppermute | solution.py:306
  64.4 1.4 %collective-permute-start.15 = (f32[3,32,512]{2,1,0:T(8,128)S(1)}, f32[3,32,512]{2,1,0:T(8,128)S(1)}, u32[]{:S(2)}, u32[]{:S(2)}) collective-permute-start(f32[3,32,512]{2,1,0:T(8,128)S(1)} %get-tuple-element.55), channel_id=1, source_target_pairs={{0,8},{8,0},{1,9},{9,1},{2,10},{10,2},{3,11},{11,3},{4,12},{12,4},... | collective-permute-start | bytes 589832 | tf_op jit(solution)/shard_map/ppermute | solution.py:305
  65.8 1.1 %collective-permute-done.15.given = f32[3,32,512]{2,1,0:T(8,128)S(1)} collective-permute-done((f32[3,32,512]{2,1,0:T(8,128)S(1)}, f32[3,32,512]{2,1,0:T(8,128)S(1)}, u32[]{:S(2)}, u32[]{:S(2)}) %collective-permute-start.15) | collective-permute-done | bytes 196640 | tf_op jit(solution)/shard_map/ppermute | solution.py:305
  66.9 2.8 %collective-permute-start.17 = (bf16[4,64,512]{2,1,0:T(8,128)(2,1)S(1)}, bf16[4,64,512]{2,1,0:T(8,128)(2,1)S(1)}, u32[]{:S(2)}, u32[]{:S(2)}) collective-permute-start(bf16[4,64,512]{2,1,0:T(8,128)(2,1)S(1)} %collective-permute-done.14.refs_1_), channel_id=1, source_target_pairs={{0,8},{8,0},{1,9},{9,1},{2,10},{10,2},{3,11},{11,3},{4,12},{12,4},... | collective-permute-start | bytes 786440 | tf_op jit(solution)/shard_map/ppermute | solution.py:320
  69.7 1.0 %shard_map.94 = (bf16[1024,1024]{1,0:T(8,128)(2,1)}, f32[32,1024]{1,0:T(8,128)}, f32[32,1024]{1,0:T(8,128)}, f32[32,1024]{1,0:T(8,128)}) custom-call(bf16[4,64,512]{2,1,0:T(8,128)(2,1)S(1)} %shard_map.93.own, bf16[4,64,512]{2,1,0:T(8,128)(2,1)S(1)} %collective-permute-done.13.arrived, f32[3,32,512]{2,1,0:T(8,128)S(1)} %get-tuple-element.54.kept, ...), custom_call_target="tpu_custom_call" | custom-call | bytes 1048576 | tf_op jit(solution)/shard_map/pallas_call | solution.py:30
  70.7 1.6 %collective-permute-start.19 = (bf16[4,64,512]{2,1,0:T(8,128)(2,1)S(1)}, bf16[4,64,512]{2,1,0:T(8,128)(2,1)S(1)}, u32[]{:S(2)}, u32[]{:S(2)}) collective-permute-start(bf16[4,64,512]{2,1,0:T(8,128)(2,1)S(1)} %collective-permute-done.18.refs_2_), channel_id=1, source_target_pairs={{0,8},{8,0},{1,9},{9,1},{2,10},{10,2},{3,11},{11,3},{4,12},{12,4},... | collective-permute-start | bytes 786440 | tf_op jit(solution)/shard_map/ppermute | solution.py:320
  (36 shorter events, 8.6 us)
Async XLA Ops:
  4.9 4.9 %collective-permute-start.1 = (bf16[512,512]{1,0:T(8,128)(2,1)S(1)}, bf16[512,512]{1,0:T(8,128)(2,1)S(1)}, u32[]{:S(2)}, u32[]{:S(2)}) collective-permute-start(bf16[512,512]{1,0:T(8,128)(2,1)S(1)} %get-tuple-element.38), channel_id=1, source_target_pairs={{0,8},{8,0},{1,9},{9,1},{2,10},{10,2},{3,11},{11,3},{4,12},{12,4},... | collective-permute-start | bytes 1572872 | tf_op jit(solution)/shard_map/ppermute | solution.py:255
  8.3 4.3 %collective-permute-start = (bf16[512,512]{1,0:T(8,128)(2,1)S(1)}, bf16[512,512]{1,0:T(8,128)(2,1)S(1)}, u32[]{:S(2)}, u32[]{:S(2)}) collective-permute-start(bf16[512,512]{1,0:T(8,128)(2,1)S(1)} %get-tuple-element.36), channel_id=1, source_target_pairs={{0,8},{8,0},{1,9},{9,1},{2,10},{10,2},{3,11},{11,3},{4,12},{12,4},... | collective-permute-start | bytes 1572872 | tf_op jit(solution)/shard_map/ppermute | solution.py:255
  9.9 7.1 %copy-start = (f32[32,1024]{1,0:T(8,128)S(1)}, f32[32,1024]{1,0:T(8,128)}, u32[]{:S(2)}) copy-start(f32[32,1024]{1,0:T(8,128)} %master) | copy-start | bytes 393220
  9.9 7.1 %copy-start.1 = (f32[32,1024]{1,0:T(8,128)S(1)}, f32[32,1024]{1,0:T(8,128)}, u32[]{:S(2)}) copy-start(f32[32,1024]{1,0:T(8,128)} %moment_one) | copy-start | bytes 393220
  10.0 7.1 %copy-start.2 = (f32[32,1024]{1,0:T(8,128)S(1)}, f32[32,1024]{1,0:T(8,128)}, u32[]{:S(2)}) copy-start(f32[32,1024]{1,0:T(8,128)} %moment_two) | copy-start | bytes 393220
  10.0 7.1 %collective-permute-start.2 = (bf16[4,64,512]{2,1,0:T(8,128)(2,1)S(1)}, bf16[4,64,512]{2,1,0:T(8,128)(2,1)S(1)}, u32[]{:S(2)}, u32[]{:S(2)}) collective-permute-start(bf16[4,64,512]{2,1,0:T(8,128)(2,1)S(1)} %get-tuple-element.39), channel_id=1, source_target_pairs={{0,32},{8,136},{16,48},{24,152},{32,0},{40,168},{48,16},{56,184},{... | collective-permute-start | bytes 786440 | tf_op jit(solution)/shard_map/ppermute | solution.py:272
  12.8 5.7 %collective-permute-start.4 = (bf16[4,64,512]{2,1,0:T(8,128)(2,1)S(1)}, bf16[4,64,512]{2,1,0:T(8,128)(2,1)S(1)}, u32[]{:S(2)}, u32[]{:S(2)}) collective-permute-start(bf16[4,64,512]{2,1,0:T(8,128)(2,1)S(1)} %get-tuple-element.41), channel_id=1, source_target_pairs={{0,16},{8,72},{16,0},{24,88},{32,48},{40,104},{48,32},{56,120},{64... | collective-permute-start | bytes 786440 | tf_op jit(solution)/shard_map/ppermute | solution.py:272
  13.2 6.7 %collective-permute-start.3 = (bf16[4,64,512]{2,1,0:T(8,128)(2,1)S(1)}, bf16[4,64,512]{2,1,0:T(8,128)(2,1)S(1)}, u32[]{:S(2)}, u32[]{:S(2)}) collective-permute-start(bf16[4,64,512]{2,1,0:T(8,128)(2,1)S(1)} %get-tuple-element.40), channel_id=1, source_target_pairs={{0,48},{8,200},{16,32},{24,216},{32,16},{40,232},{48,0},{56,248},{... | collective-permute-start | bytes 786440 | tf_op jit(solution)/shard_map/ppermute | solution.py:272
  17.1 10.6 %collective-permute-start.8 = (f32[3,32,512]{2,1,0:T(8,128)S(1)}, f32[3,32,512]{2,1,0:T(8,128)S(1)}, u32[]{:S(2)}, u32[]{:S(2)}) collective-permute-start(f32[3,32,512]{2,1,0:T(8,128)S(1)} %shard_map.91), channel_id=1, source_target_pairs={{0,8},{8,0},{1,9},{9,1},{2,10},{10,2},{3,11},{11,3},{4,12},{12,4},... | collective-permute-start | bytes 589832 | tf_op jit(solution)/shard_map/ppermute | solution.py:278
  20.1 4.7 %collective-permute-start.5 = (bf16[64,512]{1,0:T(8,128)(2,1)S(1)}, bf16[64,512]{1,0:T(8,128)(2,1)S(1)}, u32[]{:S(2)}, u32[]{:S(2)}) collective-permute-start(bf16[64,512]{1,0:T(8,128)(2,1)S(1)} %get-tuple-element.43), channel_id=1, source_target_pairs={{0,128},{8,40},{16,144},{24,56},{32,160},{40,8},{48,176},{56,24},{... | collective-permute-start | bytes 196616 | tf_op jit(solution)/shard_map/ppermute | solution.py:285
  22.7 3.4 %collective-permute-start.6 = (bf16[64,512]{1,0:T(8,128)(2,1)S(1)}, bf16[64,512]{1,0:T(8,128)(2,1)S(1)}, u32[]{:S(2)}, u32[]{:S(2)}) collective-permute-start(bf16[64,512]{1,0:T(8,128)(2,1)S(1)} %get-tuple-element.44), channel_id=1, source_target_pairs={{0,64},{8,24},{16,80},{24,8},{32,96},{40,56},{48,112},{56,40},{64,... | collective-permute-start | bytes 196616 | tf_op jit(solution)/shard_map/ppermute | solution.py:285
  23.2 4.3 %collective-permute-start.7 = (bf16[64,512]{1,0:T(8,128)(2,1)S(1)}, bf16[64,512]{1,0:T(8,128)(2,1)S(1)}, u32[]{:S(2)}, u32[]{:S(2)}) collective-permute-start(bf16[64,512]{1,0:T(8,128)(2,1)S(1)} %get-tuple-element.45), channel_id=1, source_target_pairs={{0,192},{8,56},{16,208},{24,40},{32,224},{40,24},{48,240},{56,8},{... | collective-permute-start | bytes 196616 | tf_op jit(solution)/shard_map/ppermute | solution.py:285
  53.8 4.6 %collective-permute-start.11 = (bf16[64,512]{1,0:T(8,128)(2,1)S(1)}, bf16[64,512]{1,0:T(8,128)(2,1)S(1)}, u32[]{:S(2)}, u32[]{:S(2)}) collective-permute-start(bf16[64,512]{1,0:T(8,128)(2,1)S(1)} %get-tuple-element.53.refs_0_), channel_id=1, source_target_pairs={{0,192},{8,56},{16,208},{24,40},{32,224},{40,24},{48,240},{56,8},{... | collective-permute-start | bytes 196616 | tf_op jit(solution)/shard_map/ppermute | solution.py:300
  54.7 4.6 %collective-permute-start.10 = (bf16[64,512]{1,0:T(8,128)(2,1)S(1)}, bf16[64,512]{1,0:T(8,128)(2,1)S(1)}, u32[]{:S(2)}, u32[]{:S(2)}) collective-permute-start(bf16[64,512]{1,0:T(8,128)(2,1)S(1)} %get-tuple-element.53.refs_0_), channel_id=1, source_target_pairs={{0,128},{8,40},{16,144},{24,56},{32,160},{40,8},{48,176},{56,24},{... | collective-permute-start | bytes 196616 | tf_op jit(solution)/shard_map/ppermute | solution.py:300
  56.1 3.5 %collective-permute-start.9 = (bf16[64,512]{1,0:T(8,128)(2,1)S(1)}, bf16[64,512]{1,0:T(8,128)(2,1)S(1)}, u32[]{:S(2)}, u32[]{:S(2)}) collective-permute-start(bf16[64,512]{1,0:T(8,128)(2,1)S(1)} %get-tuple-element.53.refs_0_), channel_id=1, source_target_pairs={{0,64},{8,24},{16,80},{24,8},{32,96},{40,56},{48,112},{56,40},{64,... | collective-permute-start | bytes 196616 | tf_op jit(solution)/shard_map/ppermute | solution.py:300
  59.7 7.2 %collective-permute-start.14 = (bf16[4,64,512]{2,1,0:T(8,128)(2,1)S(1)}, bf16[4,64,512]{2,1,0:T(8,128)(2,1)S(1)}, u32[]{:S(2)}, u32[]{:S(2)}) collective-permute-start(bf16[4,64,512]{2,1,0:T(8,128)(2,1)S(1)} %shard_map.93.own), channel_id=1, source_target_pairs={{0,32},{8,136},{16,48},{24,152},{32,0},{40,168},{48,16},{56,184},{... | collective-permute-start | bytes 786440 | tf_op jit(solution)/shard_map/ppermute | solution.py:306
  60.5 9.2 %collective-permute-start.13 = (bf16[4,64,512]{2,1,0:T(8,128)(2,1)S(1)}, bf16[4,64,512]{2,1,0:T(8,128)(2,1)S(1)}, u32[]{:S(2)}, u32[]{:S(2)}) collective-permute-start(bf16[4,64,512]{2,1,0:T(8,128)(2,1)S(1)} %shard_map.93.own), channel_id=1, source_target_pairs={{0,8},{8,0},{1,9},{9,1},{2,10},{10,2},{3,11},{11,3},{4,12},{12,4},... | collective-permute-start | bytes 786440 | tf_op jit(solution)/shard_map/ppermute | solution.py:309
  62.7 8.1 %collective-permute-start.12 = (bf16[4,64,512]{2,1,0:T(8,128)(2,1)S(1)}, bf16[4,64,512]{2,1,0:T(8,128)(2,1)S(1)}, u32[]{:S(2)}, u32[]{:S(2)}) collective-permute-start(bf16[4,64,512]{2,1,0:T(8,128)(2,1)S(1)} %shard_map.93.own), channel_id=1, source_target_pairs={{0,16},{8,72},{16,0},{24,88},{32,48},{40,104},{48,32},{56,120},{64... | collective-permute-start | bytes 786440 | tf_op jit(solution)/shard_map/ppermute | solution.py:306
  63.7 7.0 %collective-permute-start.18 = (bf16[4,64,512]{2,1,0:T(8,128)(2,1)S(1)}, bf16[4,64,512]{2,1,0:T(8,128)(2,1)S(1)}, u32[]{:S(2)}, u32[]{:S(2)}) collective-permute-start(bf16[4,64,512]{2,1,0:T(8,128)(2,1)S(1)} %shard_map.93.own), channel_id=1, source_target_pairs={{0,48},{8,200},{16,32},{24,216},{32,16},{40,232},{48,0},{56,248},{... | collective-permute-start | bytes 786440 | tf_op jit(solution)/shard_map/ppermute | solution.py:306
  64.4 2.5 %collective-permute-start.15 = (f32[3,32,512]{2,1,0:T(8,128)S(1)}, f32[3,32,512]{2,1,0:T(8,128)S(1)}, u32[]{:S(2)}, u32[]{:S(2)}) collective-permute-start(f32[3,32,512]{2,1,0:T(8,128)S(1)} %get-tuple-element.55), channel_id=1, source_target_pairs={{0,8},{8,0},{1,9},{9,1},{2,10},{10,2},{3,11},{11,3},{4,12},{12,4},... | collective-permute-start | bytes 589832 | tf_op jit(solution)/shard_map/ppermute | solution.py:305
  66.9 6.7 %collective-permute-start.17 = (bf16[4,64,512]{2,1,0:T(8,128)(2,1)S(1)}, bf16[4,64,512]{2,1,0:T(8,128)(2,1)S(1)}, u32[]{:S(2)}, u32[]{:S(2)}) collective-permute-start(bf16[4,64,512]{2,1,0:T(8,128)(2,1)S(1)} %collective-permute-done.14.refs_1_), channel_id=1, source_target_pairs={{0,8},{8,0},{1,9},{9,1},{2,10},{10,2},{3,11},{11,3},{4,12},{12,4},... | collective-permute-start | bytes 786440 | tf_op jit(solution)/shard_map/ppermute | solution.py:320
  70.7 2.8 %collective-permute-start.19 = (bf16[4,64,512]{2,1,0:T(8,128)(2,1)S(1)}, bf16[4,64,512]{2,1,0:T(8,128)(2,1)S(1)}, u32[]{:S(2)}, u32[]{:S(2)}) collective-permute-start(bf16[4,64,512]{2,1,0:T(8,128)(2,1)S(1)} %collective-permute-done.18.refs_2_), channel_id=1, source_target_pairs={{0,8},{8,0},{1,9},{9,1},{2,10},{10,2},{3,11},{11,3},{4,12},{12,4},... | collective-permute-start | bytes 786440 | tf_op jit(solution)/shard_map/ppermute | solution.py:320
  72.4 1.5 %collective-permute-start.16 = (bf16[4,64,512]{2,1,0:T(8,128)(2,1)S(1)}, bf16[4,64,512]{2,1,0:T(8,128)(2,1)S(1)}, u32[]{:S(2)}, u32[]{:S(2)}) collective-permute-start(bf16[4,64,512]{2,1,0:T(8,128)(2,1)S(1)} %collective-permute-done.12.refs_0_), channel_id=1, source_target_pairs={{0,8},{8,0},{1,9},{9,1},{2,10},{10,2},{3,11},{11,3},{4,12},{12,4},... | collective-permute-start | bytes 786440 | tf_op jit(solution)/shard_map/ppermute | solution.py:320
where the time goes:
time: 75.2 us; the launch traced here: 75.1 us
  starting transfers between devices  25.8 us (34%)
  blocking collectives  25.8 us (34%)
  waiting for transfers between devices  11.7 us (16%)
  Pallas kernels  10.8 us (14%)
  between operations  0.95 us (1%)
    all_to_all x1, blocking collectives, shards(): lax.all_to_all(copies, everyone, 0, 0, tiled=True).reshape(count, 128)  25.8 us
    pallas_call x13, Pallas kernels, call(): pl.pallas_call(body, out_shape=outs, in_specs=specs or [VMEM] * len(args)...  10.8 us
    ppermute x3, starting transfers between devices, shards(): others = [lax.ppermute(value, CORE, SWAP) for value in plane[1:]]  4.46 us
    ppermute x3, waiting for transfers between devices, shards(): lax.ppermute(totals[mask], DP, partners(mask, 1))  4.07 us
    ppermute x3, waiting for transfers between devices, shards(): lax.ppermute(blocks[mask], DP, partners(mask, 0))  3.61 us
    ppermute x3, starting transfers between devices, shards(): lax.ppermute(values, DP, partners(mask, 1))  3.52 us
    ppermute x2, starting transfers between devices, shards(): arrived = lax.ppermute(value, CORE, SWAP)  3.5 us
    ppermute x3, starting transfers between devices, shards(): lax.ppermute(blocks[mask], DP, partners(mask, 0))  3.43 us
  transfers between devices with their start and end apart: 20, of which 11 were waited for; matrix products, arithmetic and copies ran while one was open for 0% of the time, Pallas kernels for 7%

commit v1 on v0

--- a/solution.py
+++ b/solution.py
@@ -269,7 +269,7 @@
             *blocks,
         ]
     first = [blocks[0]] + [
-        lax.ppermute(blocks[mask], DP, partners(mask, 0)) for mask in (2, 3, 1)
+        lax.ppermute(blocks[mask], DP, partners(mask, 0)) for mask in (2, 1, 3)
     ]
     *states, _ = lax.optimization_barrier((master, moment_one, moment_two, first[1]))
     (lent,) = call(

time: 75.2 us -> 75.2 us (level)
  no operation moved by 1% of the time
where the time goes in v1:
time: 75.2 us; the launch traced here: 75.1 us
  starting transfers between devices  25.8 us (34%)
  blocking collectives  25.8 us (34%)
  waiting for transfers between devices  11.7 us (16%)
  Pallas kernels  10.8 us (14%)
  between operations  0.95 us (1%)
    all_to_all x1, blocking collectives, shards(): lax.all_to_all(copies, everyone, 0, 0, tiled=True).reshape(count, 128)  25.8 us
    pallas_call x13, Pallas kernels, call(): pl.pallas_call(body, out_shape=outs, in_specs=specs or [VMEM] * len(args)...  10.8 us
    ppermute x3, starting transfers between devices, shards(): others = [lax.ppermute(value, CORE, SWAP) for value in plane[1:]]  4.46 us
    ppermute x3, waiting for transfers between devices, shards(): lax.ppermute(totals[mask], DP, partners(mask, 1))  4.07 us
    ppermute x3, waiting for transfers between devices, shards(): lax.ppermute(blocks[mask], DP, partners(mask, 0))  3.61 us
    ppermute x3, starting transfers between devices, shards(): lax.ppermute(values, DP, partners(mask, 1))  3.52 us
    ppermute x2, starting transfers between devices, shards(): arrived = lax.ppermute(value, CORE, SWAP)  3.5 us
    ppermute x3, starting transfers between devices, shards(): lax.ppermute(blocks[mask], DP, partners(mask, 0))  3.43 us
  transfers between devices with their start and end apart: 20, of which 11 were waited for; matrix products, arithmetic and copies ran while one was open for 0% of the time, Pallas kernels for 7%

profile of v1, /device:TPU:1, one launch (start us, length us, event | category | flops | bytes accessed | tf_op | source)
XLA Modules:
  0.0 75.1 jit_solution(3798310348940118755)
XLA Ops:
  0.6 4.2 %shard_map.84 = (bf16[2048,1024]{1,0:T(8,128)(2,1)S(1)}, bf16[2048,512]{1,0:T(8,128)(2,1)S(1)}, bf16[512,512]{1,0:T(8,128)(2,1)S(1)}, bf16[512,512]{1,0:T(8,128)(2,1)S(1)}) custom-call(bf16[2048,1024]{1,0:T(8,128)(2,1)} %lg_hbm.1, bf16[2048,1024]{1,0:T(8,128)(2,1)} %hid_hbm.1), custom_call_target="tpu_custom_call" | custom-call | flops 2147483648 | bytes 8388608 | tf_op jit(solution)/shard_map/pallas_call | solution.py:30
  4.9 3.4 %collective-permute-start.1 = (bf16[512,512]{1,0:T(8,128)(2,1)S(1)}, bf16[512,512]{1,0:T(8,128)(2,1)S(1)}, u32[]{:S(2)}, u32[]{:S(2)}) collective-permute-start(bf16[512,512]{1,0:T(8,128)(2,1)S(1)} %get-tuple-element.38), channel_id=1, source_target_pairs={{0,8},{8,0},{1,9},{9,1},{2,10},{10,2},{3,11},{11,3},{4,12},{12,4},... | collective-permute-start | bytes 1572872 | tf_op jit(solution)/shard_map/ppermute | solution.py:255
  8.4 1.4 %shard_map.87.kept = bf16[512,512]{1,0:T(8,128)(2,1)S(1)} custom-call(bf16[2048,1024]{1,0:T(8,128)(2,1)S(1)} %get-tuple-element.34.lg, bf16[2048,512]{1,0:T(8,128)(2,1)S(1)} %get-tuple-element.35.hid), custom_call_target="tpu_custom_call" | custom-call | flops 1073741824 | bytes 2097152 | tf_op jit(solution)/shard_map/pallas_call | solution.py:30
  10.0 1.2 %collective-permute-start.2 = (bf16[4,64,512]{2,1,0:T(8,128)(2,1)S(1)}, bf16[4,64,512]{2,1,0:T(8,128)(2,1)S(1)}, u32[]{:S(2)}, u32[]{:S(2)}) collective-permute-start(bf16[4,64,512]{2,1,0:T(8,128)(2,1)S(1)} %get-tuple-element.39), channel_id=1, source_target_pairs={{0,32},{8,136},{16,48},{24,152},{32,0},{40,168},{48,16},{56,184},{... | collective-permute-start | bytes 786440 | tf_op jit(solution)/shard_map/ppermute | solution.py:272
  11.2 1.4 %shard_map.85.kept = bf16[512,512]{1,0:T(8,128)(2,1)S(1)} custom-call(bf16[2048,1024]{1,0:T(8,128)(2,1)S(1)} %get-tuple-element.34.lg, bf16[2048,512]{1,0:T(8,128)(2,1)S(1)} %get-tuple-element.35.hid), custom_call_target="tpu_custom_call" | custom-call | flops 1073741824 | bytes 2097152 | tf_op jit(solution)/shard_map/pallas_call | solution.py:30
  13.2 1.7 %collective-permute-start.4 = (bf16[4,64,512]{2,1,0:T(8,128)(2,1)S(1)}, bf16[4,64,512]{2,1,0:T(8,128)(2,1)S(1)}, u32[]{:S(2)}, u32[]{:S(2)}) collective-permute-start(bf16[4,64,512]{2,1,0:T(8,128)(2,1)S(1)} %get-tuple-element.41), channel_id=1, source_target_pairs={{0,48},{8,200},{16,32},{24,216},{32,16},{40,232},{48,0},{56,248},{... | collective-permute-start | bytes 786440 | tf_op jit(solution)/shard_map/ppermute | solution.py:272
  14.9 2.1 %collective-permute-done.2.one = bf16[4,64,512]{2,1,0:T(8,128)(2,1)S(1)} collective-permute-done((bf16[4,64,512]{2,1,0:T(8,128)(2,1)S(1)}, bf16[4,64,512]{2,1,0:T(8,128)(2,1)S(1)}, u32[]{:S(2)}, u32[]{:S(2)}) %collective-permute-start.2) | collective-permute-done | bytes 262176 | tf_op jit(solution)/shard_map/ppermute | solution.py:272
  17.1 1.4 %collective-permute-start.8 = (f32[3,32,512]{2,1,0:T(8,128)S(1)}, f32[3,32,512]{2,1,0:T(8,128)S(1)}, u32[]{:S(2)}, u32[]{:S(2)}) collective-permute-start(f32[3,32,512]{2,1,0:T(8,128)S(1)} %shard_map.91), channel_id=1, source_target_pairs={{0,8},{8,0},{1,9},{9,1},{2,10},{10,2},{3,11},{11,3},{4,12},{12,4},... | collective-permute-start | bytes 589832 | tf_op jit(solution)/shard_map/ppermute | solution.py:278
  18.5 1.5 %collective-permute-done.4.three = bf16[4,64,512]{2,1,0:T(8,128)(2,1)S(1)} collective-permute-done((bf16[4,64,512]{2,1,0:T(8,128)(2,1)S(1)}, bf16[4,64,512]{2,1,0:T(8,128)(2,1)S(1)}, u32[]{:S(2)}, u32[]{:S(2)}) %collective-permute-start.4) | collective-permute-done | bytes 262176 | tf_op jit(solution)/shard_map/ppermute | solution.py:272
  20.1 2.6 %collective-permute-start.5 = (bf16[64,512]{1,0:T(8,128)(2,1)S(1)}, bf16[64,512]{1,0:T(8,128)(2,1)S(1)}, u32[]{:S(2)}, u32[]{:S(2)}) collective-permute-start(bf16[64,512]{1,0:T(8,128)(2,1)S(1)} %get-tuple-element.43), channel_id=1, source_target_pairs={{0,128},{8,40},{16,144},{24,56},{32,160},{40,8},{48,176},{56,24},{... | collective-permute-start | bytes 196616 | tf_op jit(solution)/shard_map/ppermute | solution.py:285
  23.5 1.3 %collective-permute-done.5.one = bf16[64,512]{1,0:T(8,128)(2,1)S(1)} collective-permute-done((bf16[64,512]{1,0:T(8,128)(2,1)S(1)}, bf16[64,512]{1,0:T(8,128)(2,1)S(1)}, u32[]{:S(2)}, u32[]{:S(2)}) %collective-permute-start.5) | collective-permute-done | bytes 65568 | tf_op jit(solution)/shard_map/ppermute | solution.py:285
  24.8 1.3 %collective-permute-done.6.two = bf16[64,512]{1,0:T(8,128)(2,1)S(1)} collective-permute-done((bf16[64,512]{1,0:T(8,128)(2,1)S(1)}, bf16[64,512]{1,0:T(8,128)(2,1)S(1)}, u32[]{:S(2)}, u32[]{:S(2)}) %collective-permute-start.6) | collective-permute-done | bytes 65568 | tf_op jit(solution)/shard_map/ppermute | solution.py:285
  26.1 1.5 %collective-permute-done.7.three = bf16[64,512]{1,0:T(8,128)(2,1)S(1)} collective-permute-done((bf16[64,512]{1,0:T(8,128)(2,1)S(1)}, bf16[64,512]{1,0:T(8,128)(2,1)S(1)}, u32[]{:S(2)}, u32[]{:S(2)}) %collective-permute-start.7) | collective-permute-done | bytes 65568 | tf_op jit(solution)/shard_map/ppermute | solution.py:285
  27.7 25.8 %all_to_all.5 = f32[256,1,128]{2,1,0:T(1,128)S(1)} all-to-all(f32[256,1,128]{2,1,0:T(1,128)S(1)} %get-tuple-element.50), channel_id=1, replica_groups=mesh['dp_0'=4,'dp_1'=4,'dp_2'=2,'fsdp'=8] {'dp_0','dp_1','dp_2','fsdp'}, dimensions={0} | all-to-all | bytes 262144 | tf_op jit(solution)/shard_map/all_to_all | solution.py:293
  54.7 1.4 %collective-permute-start.10 = (bf16[64,512]{1,0:T(8,128)(2,1)S(1)}, bf16[64,512]{1,0:T(8,128)(2,1)S(1)}, u32[]{:S(2)}, u32[]{:S(2)}) collective-permute-start(bf16[64,512]{1,0:T(8,128)(2,1)S(1)} %get-tuple-element.53.refs_0_), channel_id=1, source_target_pairs={{0,128},{8,40},{16,144},{24,56},{32,160},{40,8},{48,176},{56,24},{... | collective-permute-start | bytes 196616 | tf_op jit(solution)/shard_map/ppermute | solution.py:300
  56.1 1.2 %collective-permute-start.9 = (bf16[64,512]{1,0:T(8,128)(2,1)S(1)}, bf16[64,512]{1,0:T(8,128)(2,1)S(1)}, u32[]{:S(2)}, u32[]{:S(2)}) collective-permute-start(bf16[64,512]{1,0:T(8,128)(2,1)S(1)} %get-tuple-element.53.refs_0_), channel_id=1, source_target_pairs={{0,64},{8,24},{16,80},{24,8},{32,96},{40,56},{48,112},{56,40},{64,... | collective-permute-start | bytes 196616 | tf_op jit(solution)/shard_map/ppermute | solution.py:300
  57.3 1.1 %collective-permute-done.11.refs_3_ = bf16[64,512]{1,0:T(8,128)(2,1)S(1)} collective-permute-done((bf16[64,512]{1,0:T(8,128)(2,1)S(1)}, bf16[64,512]{1,0:T(8,128)(2,1)S(1)}, u32[]{:S(2)}, u32[]{:S(2)}) %collective-permute-start.11) | collective-permute-done | bytes 65568 | tf_op jit(solution)/shard_map/ppermute | solution.py:300
  60.5 2.1 %collective-permute-start.13 = (bf16[4,64,512]{2,1,0:T(8,128)(2,1)S(1)}, bf16[4,64,512]{2,1,0:T(8,128)(2,1)S(1)}, u32[]{:S(2)}, u32[]{:S(2)}) collective-permute-start(bf16[4,64,512]{2,1,0:T(8,128)(2,1)S(1)} %shard_map.93.own), channel_id=1, source_target_pairs={{0,8},{8,0},{1,9},{9,1},{2,10},{10,2},{3,11},{11,3},{4,12},{12,4},... | collective-permute-start | bytes 786440 | tf_op jit(solution)/shard_map/ppermute | solution.py:309
  62.7 1.0 %collective-permute-start.12 = (bf16[4,64,512]{2,1,0:T(8,128)(2,1)S(1)}, bf16[4,64,512]{2,1,0:T(8,128)(2,1)S(1)}, u32[]{:S(2)}, u32[]{:S(2)}) collective-permute-start(bf16[4,64,512]{2,1,0:T(8,128)(2,1)S(1)} %shard_map.93.own), channel_id=1, source_target_pairs={{0,16},{8,72},{16,0},{24,88},{32,48},{40,104},{48,32},{56,120},{64... | collective-permute-start | bytes 786440 | tf_op jit(solution)/shard_map/ppermute | solution.py:306
  64.4 1.4 %collective-permute-start.15 = (f32[3,32,512]{2,1,0:T(8,128)S(1)}, f32[3,32,512]{2,1,0:T(8,128)S(1)}, u32[]{:S(2)}, u32[]{:S(2)}) collective-permute-start(f32[3,32,512]{2,1,0:T(8,128)S(1)} %get-tuple-element.55), channel_id=1, source_target_pairs={{0,8},{8,0},{1,9},{9,1},{2,10},{10,2},{3,11},{11,3},{4,12},{12,4},... | collective-permute-start | bytes 589832 | tf_op jit(solution)/shard_map/ppermute | solution.py:305
  65.8 1.1 %collective-permute-done.15.given = f32[3,32,512]{2,1,0:T(8,128)S(1)} collective-permute-done((f32[3,32,512]{2,1,0:T(8,128)S(1)}, f32[3,32,512]{2,1,0:T(8,128)S(1)}, u32[]{:S(2)}, u32[]{:S(2)}) %collective-permute-start.15) | collective-permute-done | bytes 196640 | tf_op jit(solution)/shard_map/ppermute | solution.py:305
  66.9 2.8 %collective-permute-start.17 = (bf16[4,64,512]{2,1,0:T(8,128)(2,1)S(1)}, bf16[4,64,512]{2,1,0:T(8,128)(2,1)S(1)}, u32[]{:S(2)}, u32[]{:S(2)}) collective-permute-start(bf16[4,64,512]{2,1,0:T(8,128)(2,1)S(1)} %collective-permute-done.14.refs_1_), channel_id=1, source_target_pairs={{0,8},{8,0},{1,9},{9,1},{2,10},{10,2},{3,11},{11,3},{4,12},{12,4},... | collective-permute-start | bytes 786440 | tf_op jit(solution)/shard_map/ppermute | solution.py:320
  69.7 1.0 %shard_map.94 = (bf16[1024,1024]{1,0:T(8,128)(2,1)}, f32[32,1024]{1,0:T(8,128)}, f32[32,1024]{1,0:T(8,128)}, f32[32,1024]{1,0:T(8,128)}) custom-call(bf16[4,64,512]{2,1,0:T(8,128)(2,1)S(1)} %shard_map.93.own, bf16[4,64,512]{2,1,0:T(8,128)(2,1)S(1)} %collective-permute-done.13.arrived, f32[3,32,512]{2,1,0:T(8,128)S(1)} %get-tuple-element.54.kept, ...), custom_call_target="tpu_custom_call" | custom-call | bytes 1048576 | tf_op jit(solution)/shard_map/pallas_call | solution.py:30
  70.7 1.6 %collective-permute-start.19 = (bf16[4,64,512]{2,1,0:T(8,128)(2,1)S(1)}, bf16[4,64,512]{2,1,0:T(8,128)(2,1)S(1)}, u32[]{:S(2)}, u32[]{:S(2)}) collective-permute-start(bf16[4,64,512]{2,1,0:T(8,128)(2,1)S(1)} %collective-permute-done.18.refs_2_), channel_id=1, source_target_pairs={{0,8},{8,0},{1,9},{9,1},{2,10},{10,2},{3,11},{11,3},{4,12},{12,4},... | collective-permute-start | bytes 786440 | tf_op jit(solution)/shard_map/ppermute | solution.py:320
  (36 shorter events, 8.6 us)
Async XLA Ops:
  4.9 4.9 %collective-permute-start.1 = (bf16[512,512]{1,0:T(8,128)(2,1)S(1)}, bf16[512,512]{1,0:T(8,128)(2,1)S(1)}, u32[]{:S(2)}, u32[]{:S(2)}) collective-permute-start(bf16[512,512]{1,0:T(8,128)(2,1)S(1)} %get-tuple-element.38), channel_id=1, source_target_pairs={{0,8},{8,0},{1,9},{9,1},{2,10},{10,2},{3,11},{11,3},{4,12},{12,4},... | collective-permute-start | bytes 1572872 | tf_op jit(solution)/shard_map/ppermute | solution.py:255
  8.3 4.3 %collective-permute-start = (bf16[512,512]{1,0:T(8,128)(2,1)S(1)}, bf16[512,512]{1,0:T(8,128)(2,1)S(1)}, u32[]{:S(2)}, u32[]{:S(2)}) collective-permute-start(bf16[512,512]{1,0:T(8,128)(2,1)S(1)} %get-tuple-element.36), channel_id=1, source_target_pairs={{0,8},{8,0},{1,9},{9,1},{2,10},{10,2},{3,11},{11,3},{4,12},{12,4},... | collective-permute-start | bytes 1572872 | tf_op jit(solution)/shard_map/ppermute | solution.py:255
  9.9 7.1 %copy-start = (f32[32,1024]{1,0:T(8,128)S(1)}, f32[32,1024]{1,0:T(8,128)}, u32[]{:S(2)}) copy-start(f32[32,1024]{1,0:T(8,128)} %master) | copy-start | bytes 393220
  9.9 7.1 %copy-start.1 = (f32[32,1024]{1,0:T(8,128)S(1)}, f32[32,1024]{1,0:T(8,128)}, u32[]{:S(2)}) copy-start(f32[32,1024]{1,0:T(8,128)} %moment_one) | copy-start | bytes 393220
  10.0 7.1 %copy-start.2 = (f32[32,1024]{1,0:T(8,128)S(1)}, f32[32,1024]{1,0:T(8,128)}, u32[]{:S(2)}) copy-start(f32[32,1024]{1,0:T(8,128)} %moment_two) | copy-start | bytes 393220
  10.0 7.1 %collective-permute-start.2 = (bf16[4,64,512]{2,1,0:T(8,128)(2,1)S(1)}, bf16[4,64,512]{2,1,0:T(8,128)(2,1)S(1)}, u32[]{:S(2)}, u32[]{:S(2)}) collective-permute-start(bf16[4,64,512]{2,1,0:T(8,128)(2,1)S(1)} %get-tuple-element.39), channel_id=1, source_target_pairs={{0,32},{8,136},{16,48},{24,152},{32,0},{40,168},{48,16},{56,184},{... | collective-permute-start | bytes 786440 | tf_op jit(solution)/shard_map/ppermute | solution.py:272
  12.8 5.7 %collective-permute-start.3 = (bf16[4,64,512]{2,1,0:T(8,128)(2,1)S(1)}, bf16[4,64,512]{2,1,0:T(8,128)(2,1)S(1)}, u32[]{:S(2)}, u32[]{:S(2)}) collective-permute-start(bf16[4,64,512]{2,1,0:T(8,128)(2,1)S(1)} %get-tuple-element.40), channel_id=1, source_target_pairs={{0,16},{8,72},{16,0},{24,88},{32,48},{40,104},{48,32},{56,120},{64... | collective-permute-start | bytes 786440 | tf_op jit(solution)/shard_map/ppermute | solution.py:272
  13.2 6.7 %collective-permute-start.4 = (bf16[4,64,512]{2,1,0:T(8,128)(2,1)S(1)}, bf16[4,64,512]{2,1,0:T(8,128)(2,1)S(1)}, u32[]{:S(2)}, u32[]{:S(2)}) collective-permute-start(bf16[4,64,512]{2,1,0:T(8,128)(2,1)S(1)} %get-tuple-element.41), channel_id=1, source_target_pairs={{0,48},{8,200},{16,32},{24,216},{32,16},{40,232},{48,0},{56,248},{... | collective-permute-start | bytes 786440 | tf_op jit(solution)/shard_map/ppermute | solution.py:272
  17.1 10.6 %collective-permute-start.8 = (f32[3,32,512]{2,1,0:T(8,128)S(1)}, f32[3,32,512]{2,1,0:T(8,128)S(1)}, u32[]{:S(2)}, u32[]{:S(2)}) collective-permute-start(f32[3,32,512]{2,1,0:T(8,128)S(1)} %shard_map.91), channel_id=1, source_target_pairs={{0,8},{8,0},{1,9},{9,1},{2,10},{10,2},{3,11},{11,3},{4,12},{12,4},... | collective-permute-start | bytes 589832 | tf_op jit(solution)/shard_map/ppermute | solution.py:278
  20.1 4.7 %collective-permute-start.5 = (bf16[64,512]{1,0:T(8,128)(2,1)S(1)}, bf16[64,512]{1,0:T(8,128)(2,1)S(1)}, u32[]{:S(2)}, u32[]{:S(2)}) collective-permute-start(bf16[64,512]{1,0:T(8,128)(2,1)S(1)} %get-tuple-element.43), channel_id=1, source_target_pairs={{0,128},{8,40},{16,144},{24,56},{32,160},{40,8},{48,176},{56,24},{... | collective-permute-start | bytes 196616 | tf_op jit(solution)/shard_map/ppermute | solution.py:285
  22.7 3.4 %collective-permute-start.6 = (bf16[64,512]{1,0:T(8,128)(2,1)S(1)}, bf16[64,512]{1,0:T(8,128)(2,1)S(1)}, u32[]{:S(2)}, u32[]{:S(2)}) collective-permute-start(bf16[64,512]{1,0:T(8,128)(2,1)S(1)} %get-tuple-element.44), channel_id=1, source_target_pairs={{0,64},{8,24},{16,80},{24,8},{32,96},{40,56},{48,112},{56,40},{64,... | collective-permute-start | bytes 196616 | tf_op jit(solution)/shard_map/ppermute | solution.py:285
  23.2 4.3 %collective-permute-start.7 = (bf16[64,512]{1,0:T(8,128)(2,1)S(1)}, bf16[64,512]{1,0:T(8,128)(2,1)S(1)}, u32[]{:S(2)}, u32[]{:S(2)}) collective-permute-start(bf16[64,512]{1,0:T(8,128)(2,1)S(1)} %get-tuple-element.45), channel_id=1, source_target_pairs={{0,192},{8,56},{16,208},{24,40},{32,224},{40,24},{48,240},{56,8},{... | collective-permute-start | bytes 196616 | tf_op jit(solution)/shard_map/ppermute | solution.py:285
  53.8 4.6 %collective-permute-start.11 = (bf16[64,512]{1,0:T(8,128)(2,1)S(1)}, bf16[64,512]{1,0:T(8,128)(2,1)S(1)}, u32[]{:S(2)}, u32[]{:S(2)}) collective-permute-start(bf16[64,512]{1,0:T(8,128)(2,1)S(1)} %get-tuple-element.53.refs_0_), channel_id=1, source_target_pairs={{0,192},{8,56},{16,208},{24,40},{32,224},{40,24},{48,240},{56,8},{... | collective-permute-start | bytes 196616 | tf_op jit(solution)/shard_map/ppermute | solution.py:300
  54.7 4.6 %collective-permute-start.10 = (bf16[64,512]{1,0:T(8,128)(2,1)S(1)}, bf16[64,512]{1,0:T(8,128)(2,1)S(1)}, u32[]{:S(2)}, u32[]{:S(2)}) collective-permute-start(bf16[64,512]{1,0:T(8,128)(2,1)S(1)} %get-tuple-element.53.refs_0_), channel_id=1, source_target_pairs={{0,128},{8,40},{16,144},{24,56},{32,160},{40,8},{48,176},{56,24},{... | collective-permute-start | bytes 196616 | tf_op jit(solution)/shard_map/ppermute | solution.py:300
  56.1 3.5 %collective-permute-start.9 = (bf16[64,512]{1,0:T(8,128)(2,1)S(1)}, bf16[64,512]{1,0:T(8,128)(2,1)S(1)}, u32[]{:S(2)}, u32[]{:S(2)}) collective-permute-start(bf16[64,512]{1,0:T(8,128)(2,1)S(1)} %get-tuple-element.53.refs_0_), channel_id=1, source_target_pairs={{0,64},{8,24},{16,80},{24,8},{32,96},{40,56},{48,112},{56,40},{64,... | collective-permute-start | bytes 196616 | tf_op jit(solution)/shard_map/ppermute | solution.py:300
  59.7 7.2 %collective-permute-start.14 = (bf16[4,64,512]{2,1,0:T(8,128)(2,1)S(1)}, bf16[4,64,512]{2,1,0:T(8,128)(2,1)S(1)}, u32[]{:S(2)}, u32[]{:S(2)}) collective-permute-start(bf16[4,64,512]{2,1,0:T(8,128)(2,1)S(1)} %shard_map.93.own), channel_id=1, source_target_pairs={{0,32},{8,136},{16,48},{24,152},{32,0},{40,168},{48,16},{56,184},{... | collective-permute-start | bytes 786440 | tf_op jit(solution)/shard_map/ppermute | solution.py:306
  60.5 9.2 %collective-permute-start.13 = (bf16[4,64,512]{2,1,0:T(8,128)(2,1)S(1)}, bf16[4,64,512]{2,1,0:T(8,128)(2,1)S(1)}, u32[]{:S(2)}, u32[]{:S(2)}) collective-permute-start(bf16[4,64,512]{2,1,0:T(8,128)(2,1)S(1)} %shard_map.93.own), channel_id=1, source_target_pairs={{0,8},{8,0},{1,9},{9,1},{2,10},{10,2},{3,11},{11,3},{4,12},{12,4},... | collective-permute-start | bytes 786440 | tf_op jit(solution)/shard_map/ppermute | solution.py:309
  62.7 8.1 %collective-permute-start.12 = (bf16[4,64,512]{2,1,0:T(8,128)(2,1)S(1)}, bf16[4,64,512]{2,1,0:T(8,128)(2,1)S(1)}, u32[]{:S(2)}, u32[]{:S(2)}) collective-permute-start(bf16[4,64,512]{2,1,0:T(8,128)(2,1)S(1)} %shard_map.93.own), channel_id=1, source_target_pairs={{0,16},{8,72},{16,0},{24,88},{32,48},{40,104},{48,32},{56,120},{64... | collective-permute-start | bytes 786440 | tf_op jit(solution)/shard_map/ppermute | solution.py:306
  63.7 7.0 %collective-permute-start.18 = (bf16[4,64,512]{2,1,0:T(8,128)(2,1)S(1)}, bf16[4,64,512]{2,1,0:T(8,128)(2,1)S(1)}, u32[]{:S(2)}, u32[]{:S(2)}) collective-permute-start(bf16[4,64,512]{2,1,0:T(8,128)(2,1)S(1)} %shard_map.93.own), channel_id=1, source_target_pairs={{0,48},{8,200},{16,32},{24,216},{32,16},{40,232},{48,0},{56,248},{... | collective-permute-start | bytes 786440 | tf_op jit(solution)/shard_map/ppermute | solution.py:306
  64.4 2.5 %collective-permute-start.15 = (f32[3,32,512]{2,1,0:T(8,128)S(1)}, f32[3,32,512]{2,1,0:T(8,128)S(1)}, u32[]{:S(2)}, u32[]{:S(2)}) collective-permute-start(f32[3,32,512]{2,1,0:T(8,128)S(1)} %get-tuple-element.55), channel_id=1, source_target_pairs={{0,8},{8,0},{1,9},{9,1},{2,10},{10,2},{3,11},{11,3},{4,12},{12,4},... | collective-permute-start | bytes 589832 | tf_op jit(solution)/shard_map/ppermute | solution.py:305
  66.9 6.7 %collective-permute-start.17 = (bf16[4,64,512]{2,1,0:T(8,128)(2,1)S(1)}, bf16[4,64,512]{2,1,0:T(8,128)(2,1)S(1)}, u32[]{:S(2)}, u32[]{:S(2)}) collective-permute-start(bf16[4,64,512]{2,1,0:T(8,128)(2,1)S(1)} %collective-permute-done.14.refs_1_), channel_id=1, source_target_pairs={{0,8},{8,0},{1,9},{9,1},{2,10},{10,2},{3,11},{11,3},{4,12},{12,4},... | collective-permute-start | bytes 786440 | tf_op jit(solution)/shard_map/ppermute | solution.py:320
  70.7 2.8 %collective-permute-start.19 = (bf16[4,64,512]{2,1,0:T(8,128)(2,1)S(1)}, bf16[4,64,512]{2,1,0:T(8,128)(2,1)S(1)}, u32[]{:S(2)}, u32[]{:S(2)}) collective-permute-start(bf16[4,64,512]{2,1,0:T(8,128)(2,1)S(1)} %collective-permute-done.18.refs_2_), channel_id=1, source_target_pairs={{0,8},{8,0},{1,9},{9,1},{2,10},{10,2},{3,11},{11,3},{4,12},{12,4},... | collective-permute-start | bytes 786440 | tf_op jit(solution)/shard_map/ppermute | solution.py:320
  72.4 1.5 %collective-permute-start.16 = (bf16[4,64,512]{2,1,0:T(8,128)(2,1)S(1)}, bf16[4,64,512]{2,1,0:T(8,128)(2,1)S(1)}, u32[]{:S(2)}, u32[]{:S(2)}) collective-permute-start(bf16[4,64,512]{2,1,0:T(8,128)(2,1)S(1)} %collective-permute-done.12.refs_0_), channel_id=1, source_target_pairs={{0,8},{8,0},{1,9},{9,1},{2,10},{10,2},{3,11},{11,3},{4,12},{12,4},... | collective-permute-start | bytes 786440 | tf_op jit(solution)/shard_map/ppermute | solution.py:320
